TPU v7x, 32 devices: a whole 2x2x4 slice. The times are simulated.
32 devices in a mesh: panel: 4 (over y, core), blk: 8 (over z, x).
Axes of the slice: x: 2, y: 2, z: 4, core: 2. Of those that a mesh axis runs over, the one named last changes fastest.
Arguments:
- source_flux: bfloat16 [72, 256, 1024], P(None, 'panel', 'blk'), may hold values from -6 to 6
- gauss_weight: float32 [4, 256, 512], P(None, ('panel', 'blk')), may hold values from 0.02 to 0.2
- gauss_offset: float32 [2, 4, 256, 512], P(None, None, ('panel', 'blk')), may hold values from -0.5 to 0.5
- slot_count: int32 [256], P(('panel', 'blk')), may hold values from 1 to 512, as said below
- source_cell: int32 [256, 512], P(('panel', 'blk')), may hold values from 0 to 8191, as said below
- target_cell: int32 [256, 512], P(('panel', 'blk')), may hold values from 0 to 4095, as said below
- target_area: float32 [131072], P(('panel', 'blk')), may hold values from 0.25 to 1
Outputs:
- remapped: bfloat16 [72, 131072], P(None, ('panel', 'blk'))
Inputs may be any that keep to these rules, and one draw needn't show every extreme that they name: `slot_count`: live slots from source s to owner k of its band at entry s * size of blk + k; in every draw some owner receives 512 live slots from every source device of its band. `source_cell`: Row-major index of a cell in the sender's block of 64 x 128; slots past the count hold arbitrary cells. `target_cell`: cell index within owner d's 4096 cells; row d * size of blk + k lists the slots from source k of d's band.
All inputs are finite; a program needn't handle non-finite values.
Results may differ from a plain program's by a relative error of at most 0.0044.
The roundings to bfloat16 on the way count: a program that leaves them out, or rounds other values in their place, can miss the bound.
Values may be sent and summed in bfloat16 or wider, within the bound.
A program may use at most 192 MiB of HBM per device.

v0:
```python
import jax
import jax.numpy as jnp
import numpy as np
from jax import lax
from jax.experimental import pallas as pl
from jax.experimental.pallas import tpu as pltpu
from jax.sharding import PartitionSpec as P

LANES = 128
GROUP = 16
TAPS = 16
LEFT = 8
PARTS = 3
LOW = 256


def tap_pattern():
    first = np.array([1, -8, 0, 8, -1, 0, 0, 0])
    second = np.array([-1, 16, -30, 16, -1, 0, 0, 0])
    here = np.array([0, 0, 1, 0, 0, 0, 0, 0])
    none = np.zeros(8)
    rows = [
        np.concatenate([here, none]),
        np.concatenate([none, first]),
        np.concatenate([first, none]),
        np.concatenate([none, second]),
        np.concatenate([second, none]),
    ]
    rows += [np.zeros(TAPS)] * 3
    return np.tile(np.stack(rows), (PARTS, GROUP)).astype(np.float32)


def gather_kernel(
    count, cells, flux, above, below, before, after, weight, offset, pattern, out, wide, grid, mom
):
    fields, height, breadth = flux.shape
    members, capacity = cells.shape
    pitch = breadth + 2 * LEFT
    chunks = capacity // LANES
    shift = breadth.bit_length() - 1
    assert breadth == 1 << shift
    fill = jnp.zeros((LANES - fields, breadth), jnp.float32)

    grid[...] = jnp.zeros_like(grid)

    def widen(f, carry):
        wide[pl.ds(f * height, height), :] = flux[f].astype(jnp.float32)
        return carry

    lax.fori_loop(0, fields, widen, 0, unroll=8)

    def place(row, block):
        turned = jnp.concatenate([block, fill], axis=0).T
        grid[pl.ds(pl.multiple_of(row * pitch + LEFT, 8), breadth), :] = turned

    for r in range(2):
        place(r, above[r].astype(jnp.float32))
        place(height + 2 + r, below[r].astype(jnp.float32))

    def turn(i, carry):
        place(i + 2, wide[pl.ds(i, fields, stride=height), :])
        return carry

    lax.fori_loop(0, height, turn, 0, unroll=4)
    for q in range(2):
        grid[pl.ds(2 * pitch + LEFT - 2 + q, height, stride=pitch), :] = before[q].astype(jnp.float32)
        grid[pl.ds(2 * pitch + LEFT + breadth + q, height, stride=pitch), :] = after[q].astype(
            jnp.float32
        )

    w = weight[...]
    ox = offset[0]
    oy = offset[1]
    moments = [
        jnp.sum(w, axis=0),
        jnp.sum(w * ox, axis=0) / 12.0,
        jnp.sum(w * oy, axis=0) / 12.0,
        0.5 * jnp.sum(w * ox * ox, axis=0) / 12.0,
        0.5 * jnp.sum(w * oy * oy, axis=0) / 12.0,
    ]
    mom[...] = jnp.zeros_like(mom)
    slots = lax.broadcasted_iota(jnp.int32, (1, capacity), 1)
    alive = [slots < count[k] for k in range(members)]
    for m, moment in enumerate(moments):
        for part in range(PARTS):
            piece = moment.astype(jnp.bfloat16).astype(jnp.float32)
            moment = moment - piece
            for k in range(members):
                mom[k, part * 8 + m : part * 8 + m + 1, :] = jnp.where(alive[k], piece[k : k + 1, :], 0.0)

    slot_group = lax.broadcasted_iota(jnp.int32, (LANES, GROUP * TAPS), 0) % GROUP
    tap_group = lax.broadcasted_iota(jnp.int32, (LANES, GROUP * TAPS), 1) // TAPS
    diagonal = slot_group == tap_group

    def chunk(step, carry):
        k = step // chunks
        q = step % chunks
        start = pl.multiple_of(q * LANES, LANES)
        live = count[k] - start

        @pl.when(live > 0)
        def _():
            m = mom[k, :, pl.ds(start, LANES)].T.astype(jnp.bfloat16)
            coef = jnp.dot(m, pattern[...], preferred_element_type=jnp.float32)
            coef = jnp.where(diagonal, coef, 0.0)
            high = coef.astype(jnp.bfloat16)
            low = (coef - high.astype(jnp.float32)).astype(jnp.bfloat16)
            parts = []
            for g in range(LANES // GROUP):
                taps = []
                for s in range(GROUP):
                    cell = cells[k, start + g * GROUP + s]
                    base = cell + lax.shift_right_logical(cell, shift) * (pitch - breadth)
                    taps.append(grid[pl.ds(base + 2 * pitch + LEFT - 2, 8), :])
                    taps.append(grid[pl.ds(base + LEFT, 8, stride=pitch), :])
                picked = jnp.concatenate(taps, axis=0).astype(jnp.bfloat16)
                rows = slice(g * GROUP, (g + 1) * GROUP)
                both = jnp.concatenate([high[rows], low[rows]], axis=0)
                r = jnp.dot(both, picked, preferred_element_type=jnp.float32)
                parts.append(r[:GROUP] + r[GROUP:])
            record = jnp.concatenate(parts, axis=0).T
            out[k, :, pl.ds(start, LANES)] = record[:fields].astype(jnp.bfloat16)

        @pl.when(live <= 0)
        def _():
            out[k, :, pl.ds(start, LANES)] = jnp.zeros((fields, LANES), jnp.bfloat16)

        return carry

    lax.fori_loop(0, members * chunks, chunk, 0)


def scatter_kernel(records, target, area, out, landed, masked, total, sent, came):
    members, fields, capacity = records.shape
    digits = out.shape[1] // LOW
    rows = total.shape[0] // digits
    fill = jnp.zeros((rows - fields, capacity), jnp.bfloat16)
    me = lax.axis_index("blk")

    def peer(step):
        return {"blk": lax.rem(me + step, members)}

    def copy(step):
        return pltpu.make_async_remote_copy(
            src_ref=records.at[lax.rem(me + step, members)],
            dst_ref=landed.at[step - 1],
            send_sem=sent.at[step - 1],
            recv_sem=came.at[step - 1],
            device_id=peer(step),
            device_id_type=pl.DeviceIdType.MESH,
        )

    barrier = pltpu.get_barrier_semaphore()
    for step in range(1, members):
        pl.semaphore_signal(barrier, 1, device_id=peer(step), device_id_type=pl.DeviceIdType.MESH)
    pl.semaphore_wait(barrier, members - 1)
    for step in range(1, members):
        copy(step).start()

    def deposit(record, source):
        cell = target[pl.ds(source, 1), :]
        high = lax.shift_right_logical(cell, LOW.bit_length() - 1)
        low = cell & (LOW - 1)
        spots = lax.broadcasted_iota(jnp.int32, (LOW, capacity), 0)
        table = jnp.where(spots == low, 1.0, 0.0).astype(jnp.bfloat16)
        record = jnp.concatenate([record, fill], axis=0)
        for h in range(digits):
            here = jnp.where(high == h, 1.0, 0.0).astype(jnp.bfloat16)
            masked[h * rows : (h + 1) * rows, :] = record * here
        return lax.dot_general(
            masked[...], table, (((1,), (1,)), ((), ())), preferred_element_type=jnp.float32
        )

    total[...] = deposit(records[me], me)

    def arrival(step, carry):
        copy(step).wait_recv()
        total[...] += deposit(landed[step - 1], lax.rem(me - step + members, members))
        return carry

    lax.fori_loop(1, members, arrival, 0)
    for h in range(digits):
        columns = slice(h * LOW, (h + 1) * LOW)
        value = total[h * rows : h * rows + fields, :] / area[:, columns]
        out[:, columns] = value.astype(jnp.bfloat16)
    for step in range(1, members):
        copy(step).wait_send()


def on_device(
    source_flux, gauss_weight, gauss_offset, slot_count, source_cell, target_cell, target_area
):
    fields, height, breadth = source_flux.shape
    members, capacity = source_cell.shape
    ocean_cells = target_area.shape[0]
    pitch = breadth + 2 * LEFT

    panels = lax.axis_size("panel")
    columns = lax.axis_size("blk")
    up = [(i, i + 1) for i in range(panels - 1)]
    down = [(i + 1, i) for i in range(panels - 1)]
    east = [(i, (i + 1) % columns) for i in range(columns)]
    west = [(j, i) for i, j in east]
    first_rows = jnp.transpose(source_flux[:, :2, :], (1, 0, 2))
    last_rows = jnp.transpose(source_flux[:, height - 2 :, :], (1, 0, 2))
    first_cols = jnp.transpose(source_flux[:, :, :2], (2, 1, 0))
    last_cols = jnp.transpose(source_flux[:, :, breadth - 2 :], (2, 1, 0))
    wide_lanes = ((0, 0), (0, 0), (0, LANES - fields))
    above = lax.ppermute(last_rows, "panel", up)
    below = lax.ppermute(first_rows, "panel", down)
    before = lax.ppermute(jnp.pad(last_cols, wide_lanes), "blk", east)
    after = lax.ppermute(jnp.pad(first_cols, wide_lanes), "blk", west)

    vmem = pl.BlockSpec(memory_space=pltpu.VMEM)
    smem = pl.BlockSpec(memory_space=pltpu.SMEM)
    records = pl.pallas_call(
        gather_kernel,
        out_shape=jax.ShapeDtypeStruct((members, fields, capacity), jnp.bfloat16),
        in_specs=[smem, smem] + [vmem] * 8,
        out_specs=vmem,
        scratch_shapes=[
            pltpu.VMEM((fields * height, breadth), jnp.float32),
            pltpu.VMEM(((height + 8) * pitch, LANES), jnp.float32),
            pltpu.VMEM((members, 8 * PARTS, capacity), jnp.float32),
        ],
        compiler_params=pltpu.CompilerParams(vmem_limit_bytes=48 * 2**20),
        name="gather_records",
    )(
        slot_count,
        source_cell,
        source_flux,
        above,
        below,
        before,
        after,
        gauss_weight,
        gauss_offset,
        jnp.asarray(tap_pattern(), jnp.bfloat16),
    )
    digits = ocean_cells // LOW
    rows = -(-fields // 16) * 16
    return pl.pallas_call(
        scatter_kernel,
        out_shape=jax.ShapeDtypeStruct((fields, ocean_cells), jnp.bfloat16),
        in_specs=[vmem] * 3,
        out_specs=vmem,
        scratch_shapes=[
            pltpu.VMEM((members - 1, fields, capacity), jnp.bfloat16),
            pltpu.VMEM((digits * rows, capacity), jnp.bfloat16),
            pltpu.VMEM((digits * rows, LOW), jnp.float32),
            pltpu.SemaphoreType.DMA((members - 1,)),
            pltpu.SemaphoreType.DMA((members - 1,)),
        ],
        compiler_params=pltpu.CompilerParams(
            vmem_limit_bytes=48 * 2**20, collective_id=0, has_side_effects=True
        ),
        name="scatter_records",
    )(records, target_cell, target_area.reshape(1, ocean_cells))


def solution(mesh):
    placed = (
        P(None, "panel", "blk"),
        P(None, ("panel", "blk"), None),
        P(None, None, ("panel", "blk"), None),
        P(("panel", "blk")),
        P(("panel", "blk"), None),
        P(("panel", "blk"), None),
        P(("panel", "blk")),
    )
    return jax.shard_map(
        on_device, mesh=mesh, in_specs=placed, out_specs=P(None, ("panel", "blk")), check_vma=False
    )
```

profile of v0, /device:TPU:30, one launch (start us, length us, event | category | flops | bytes accessed | tf_op | source)
XLA Modules:
  0.0 55.1 jit_solution(6778446297637553074)
XLA Ops:
  0.0 1.0 %fusion.1 = (bf16[72,2,128]{2,1,0:T(2,128)(2,1)S(1)}, bf16[72,2,128]{2,1,0:T(2,128)(2,1)S(1)}) fusion(bf16[72,64,128]{2,1,0:T(8,128)(2,1)} %flux.1), kind=kLoop, calls=%fused_computation.3 | loop fusion | bytes 147456 | tf_op jit(solution)/shard_map/slice | solution.py:204
  1.1 1.9 %collective-permute-start = (bf16[2,72,128]{2,1,0:T(8,128)(2,1)S(1)}, bf16[2,72,128]{2,1,0:T(8,128)(2,1)S(1)}, u32[]{:S(2)}, u32[]{:S(2)}) collective-permute-start(bf16[2,72,128]{2,1,0:T(8,128)(2,1)S(1)} %bitcast.12), channel_id=1, source_target_pairs={{0,8},{8,16},{16,24},{1,9},{9,17},{17,25},{2,10},{10,18},{18,26},{... | collective-permute-start | bytes 110600 | tf_op jit(solution)/shard_map/ppermute | solution.py:209
  3.0 3.6 %collective-permute-start.1 = (bf16[2,72,128]{2,1,0:T(8,128)(2,1)S(1)}, bf16[2,72,128]{2,1,0:T(8,128)(2,1)S(1)}, u32[]{:S(2)}, u32[]{:S(2)}) collective-permute-start(bf16[2,72,128]{2,1,0:T(8,128)(2,1)S(1)} %bitcast.13), channel_id=1, source_target_pairs={{8,0},{16,8},{24,16},{9,1},{17,9},{25,17},{10,2},{18,10},{26,18},{... | collective-permute-start | bytes 110600 | tf_op jit(solution)/shard_map/ppermute | solution.py:210
  6.7 3.2 %fusion = (bf16[72,64,2]{2,1,0:T(8,128)(2,1)S(1)}, bf16[72,64,2]{2,1,0:T(8,128)(2,1)}) fusion(bf16[72,64,128]{2,1,0:T(8,128)(2,1)} %flux.1), kind=kLoop, calls=%fused_computation.2 | loop fusion | bytes 73728 | tf_op jit(solution)/shard_map/slice | solution.py:206
  9.9 0.0 copy-start
  9.9 0.0 copy-start.1
  9.9 0.0 copy-start.2
  9.9 0.0 copy-start.3
  9.9 0.0 copy-start.6
  9.9 0.0 copy-start.7
  9.9 2.7 %copy.15 = bf16[72,64,2]{0,1,2:T(8,128)(2,1)S(1)} copy(bf16[72,64,2]{2,1,0:T(8,128)(2,1)} %get-tuple-element.6) | data formatting | bytes 36864
  12.7 0.2 collective-permute-start.2
  12.9 1.4 %copy.16 = bf16[72,64,2]{0,1,2:T(8,128)(2,1)S(1)} copy(bf16[72,64,2]{2,1,0:T(8,128)(2,1)S(1)} %get-tuple-element.5) | data formatting | bytes 36864
  14.3 0.0 copy-start.4
  14.3 0.0 copy-start.5
  14.3 1.9 %collective-permute-start.3 = (bf16[2,64,128]{2,1,0:T(8,128)(2,1)S(1)}, bf16[2,64,128]{2,1,0:T(8,128)(2,1)S(1)}, u32[]{:S(2)}, u32[]{:S(2)}) collective-permute-start(bf16[2,64,128]{2,1,0:T(8,128)(2,1)S(1)} %pad.8), channel_id=1, source_target_pairs={{1,0},{2,1},{3,2},{4,3},{5,4},{6,5},{7,6},{0,7},{9,8},{10,9},{11,1... | collective-permute-start | bytes 98312 | tf_op jit(solution)/shard_map/ppermute | solution.py:212
  16.2 0.4 collective-permute-done.2.before
  16.6 4.3 %collective-permute-done.3.after = bf16[2,64,128]{2,1,0:T(8,128)(2,1)S(1)} collective-permute-done((bf16[2,64,128]{2,1,0:T(8,128)(2,1)S(1)}, bf16[2,64,128]{2,1,0:T(8,128)(2,1)S(1)}, u32[]{:S(2)}, u32[]{:S(2)}) %collective-permute-start.3) | collective-permute-done | bytes 32800 | tf_op jit(solution)/shard_map/ppermute | solution.py:212
  21.0 0.0 collective-permute-done.above
  21.0 0.0 collective-permute-done.1.below
  21.0 0.0 copy-done
  21.0 0.0 copy-done.1
  21.0 0.0 copy-done.2
  21.0 0.0 copy-done.3
  21.0 0.0 copy-done.6
  21.0 0.0 copy-done.7
  21.0 19.6 %gather_records.1.records = bf16[8,72,512]{2,1,0:T(8,128)(2,1)S(1)} custom-call(s32[8]{0:T(128)S(1)} %copy-done.7, s32[8,512]{1,0:T(8,128)S(1)} %copy-done.3, bf16[72,64,128]{2,1,0:T(8,128)(2,1)S(1)} %copy-done, bf16[2,72,128]{2,1,0:T(8,128)(2,1)S(1)} %collective-permute-done.above, bf16[2,72,128]{2,1,0:T(8,128)(2,1)S(1)} %collective-permute-done.1.below, ...), custom_call_target="tpu_custom_call" | custom-call | tf_op jit(solution)/shard_map/gather_records/pallas_call | solution.py:216
  40.6 0.0 copy-done.4
  40.6 0.0 copy-done.5
  40.6 13.6 %scatter_records.1 = bf16[72,4096]{1,0:T(8,128)(2,1)S(1)} custom-call(bf16[8,72,512]{2,1,0:T(8,128)(2,1)S(1)} %gather_records.1.records, s32[8,512]{1,0:T(8,128)S(1)} %copy-done.4, f32[1,4096]{1,0:T(1,128)S(1)} %bitcast.9), custom_call_target="tpu_custom_call" | custom-call | tf_op jit(solution)/shard_map/scatter_records/pallas_call | solution.py:242
  54.3 0.8 %copy.22 = bf16[72,4096]{1,0:T(8,128)(2,1)} copy(bf16[72,4096]{1,0:T(8,128)(2,1)S(1)} %scatter_records.1) | data formatting | bytes 1179648
  (4 shorter events, 0.0 us)
Async XLA Ops:
  1.1 19.9 %collective-permute-start = (bf16[2,72,128]{2,1,0:T(8,128)(2,1)S(1)}, bf16[2,72,128]{2,1,0:T(8,128)(2,1)S(1)}, u32[]{:S(2)}, u32[]{:S(2)}) collective-permute-start(bf16[2,72,128]{2,1,0:T(8,128)(2,1)S(1)} %bitcast.12), channel_id=1, source_target_pairs={{0,8},{8,16},{16,24},{1,9},{9,17},{17,25},{2,10},{10,18},{18,26},{... | collective-permute-start | bytes 110600 | tf_op jit(solution)/shard_map/ppermute | solution.py:209
  3.0 17.9 %collective-permute-start.1 = (bf16[2,72,128]{2,1,0:T(8,128)(2,1)S(1)}, bf16[2,72,128]{2,1,0:T(8,128)(2,1)S(1)}, u32[]{:S(2)}, u32[]{:S(2)}) collective-permute-start(bf16[2,72,128]{2,1,0:T(8,128)(2,1)S(1)} %bitcast.13), channel_id=1, source_target_pairs={{8,0},{16,8},{24,16},{9,1},{17,9},{25,17},{10,2},{18,10},{26,18},{... | collective-permute-start | bytes 110600 | tf_op jit(solution)/shard_map/ppermute | solution.py:210
  9.9 11.1 %copy-start = (bf16[72,64,128]{2,1,0:T(8,128)(2,1)S(1)}, bf16[72,64,128]{2,1,0:T(8,128)(2,1)}, u32[]{:S(2)}) copy-start(bf16[72,64,128]{2,1,0:T(8,128)(2,1)} %flux.1) | copy-start | bytes 3538948
  9.9 11.1 %copy-start.1 = (f32[2,4,8,512]{3,2,1,0:T(8,128)S(1)}, f32[2,4,8,512]{3,2,1,0:T(8,128)}, u32[]{:S(2)}) copy-start(f32[2,4,8,512]{3,2,1,0:T(8,128)} %offset.1) | copy-start | bytes 393220
  9.9 11.1 %copy-start.2 = (f32[4,8,512]{2,1,0:T(8,128)S(1)}, f32[4,8,512]{2,1,0:T(8,128)}, u32[]{:S(2)}) copy-start(f32[4,8,512]{2,1,0:T(8,128)} %weight.1) | copy-start | bytes 196612
  9.9 11.1 %copy-start.3 = (s32[8,512]{1,0:T(8,128)S(1)}, s32[8,512]{1,0:T(8,128)}, u32[]{:S(2)}) copy-start(s32[8,512]{1,0:T(8,128)} %cells.1) | copy-start | bytes 49156
  9.9 11.1 %copy-start.6 = (bf16[24,256]{1,0:T(8,128)(2,1)S(1)}, bf16[24,256]{1,0:T(8,128)(2,1)}, u32[]{:S(2)}) copy-start(bf16[24,256]{1,0:T(8,128)(2,1)} %constant.5.clone.pattern) | copy-start | bytes 36868
  9.9 11.1 %copy-start.7 = (s32[8]{0:T(128)S(1)}, s32[8]{0:T(128)}, u32[]{:S(2)}) copy-start(s32[8]{0:T(128)} %count.1) | copy-start | bytes 100
  12.7 4.0 %collective-permute-start.2 = (bf16[2,64,128]{2,1,0:T(8,128)(2,1)S(1)}, bf16[2,64,128]{2,1,0:T(8,128)(2,1)S(1)}, u32[]{:S(2)}, u32[]{:S(2)}) collective-permute-start(bf16[2,64,128]{2,1,0:T(8,128)(2,1)S(1)} %pad.7), channel_id=1, source_target_pairs={{0,1},{1,2},{2,3},{3,4},{4,5},{5,6},{6,7},{7,0},{8,9},{9,10},{10,1... | collective-permute-start | bytes 98312 | tf_op jit(solution)/shard_map/ppermute | solution.py:211
  14.3 26.3 %copy-start.4 = (s32[8,512]{1,0:T(8,128)S(1)}, s32[8,512]{1,0:T(8,128)}, u32[]{:S(2)}) copy-start(s32[8,512]{1,0:T(8,128)} %target.1) | copy-start | bytes 49156
  14.3 26.3 %copy-start.5 = (f32[4096]{0:T(1024)S(1)}, f32[4096]{0:T(1024)}, u32[]{:S(2)}) copy-start(f32[4096]{0:T(1024)} %param.14) | copy-start | bytes 49156
  14.3 6.7 %collective-permute-start.3 = (bf16[2,64,128]{2,1,0:T(8,128)(2,1)S(1)}, bf16[2,64,128]{2,1,0:T(8,128)(2,1)S(1)}, u32[]{:S(2)}, u32[]{:S(2)}) collective-permute-start(bf16[2,64,128]{2,1,0:T(8,128)(2,1)S(1)} %pad.8), channel_id=1, source_target_pairs={{1,0},{2,1},{3,2},{4,3},{5,4},{6,5},{7,6},{0,7},{9,8},{10,9},{11,1... | collective-permute-start | bytes 98312 | tf_op jit(solution)/shard_map/ppermute | solution.py:212
where the time goes:
time: 56.2 us; the launch traced here: 55.1 us
  Pallas kernels  33.2 us (59%)
  local copies, waits for them, and re-layouts  9.23 us (16%)
  starting transfers between devices  7.69 us (14%)
  waiting for transfers between devices  4.78 us (9%)
    pallas_call x1, Pallas kernels, on_device(): pl.pallas_call(gather_kernel, out_shape=jax.ShapeDtypeStruct((members, fi...  19.6 us
    pallas_call x1, Pallas kernels, on_device(): pl.pallas_call(scatter_kernel, out_shape=jax.ShapeDtypeStruct((fields, oc...  13.6 us
    unnamed x21, local copies, waits for them, and re-layouts  4.96 us
    ppermute x1, waiting for transfers between devices, on_device(): after = lax.ppermute(jnp.pad(first_cols, wide_lanes), 'blk', west)  4.33 us
    ppermute x1, starting transfers between devices, on_device(): below = lax.ppermute(first_rows, 'panel', down)  3.64 us
    slice x1, local copies, waits for them, and re-layouts, on_device(): first_cols = jnp.transpose(source_flux[:, :, :2], (2, 1, 0))  3.2 us
    ppermute x1, starting transfers between devices, on_device(): above = lax.ppermute(last_rows, 'panel', up)  1.92 us
    ppermute x1, starting transfers between devices, on_device(): after = lax.ppermute(jnp.pad(first_cols, wide_lanes), 'blk', west)  1.88 us
  transfers between devices with their start and end apart: 4, of which 2 were waited for; matrix products, arithmetic and copies ran while one was open for 13% of the time, Pallas kernels for 0%

commit v1 on v0

--- a/solution.py
+++ b/solution.py
@@ -28,6 +28,81 @@
     ]
     rows += [np.zeros(TAPS)] * 3
     return np.tile(np.stack(rows), (PARTS, GROUP)).astype(np.float32)
+
+
+def halo_kernel(
+    flux, above, below, before, after, wide, edges, row_out, col_out, row_in, col_in, sent, came
+):
+    fields, height, breadth = flux.shape
+    axes = ("panel", "panel", "blk", "blk")
+    shifts = (1, -1, 1, -1)
+
+    def neighbour(n):
+        size = lax.axis_size(axes[n])
+        return {axes[n]: lax.rem(lax.axis_index(axes[n]) + shifts[n] + size, size)}
+
+    barrier = pltpu.get_barrier_semaphore()
+    for n in range(4):
+        pl.semaphore_signal(
+            barrier, 1, device_id=neighbour(n), device_id_type=pl.DeviceIdType.MESH
+        )
+
+    def widen(f, carry):
+        wide[pl.ds(f * height, height), :] = flux[f].astype(jnp.float32)
+        return carry
+
+    lax.fori_loop(0, fields, widen, 0, unroll=8)
+    for side, first in enumerate((height - 2, 0)):
+        for r in range(2):
+            row = wide[pl.ds(first + r, fields, stride=height), :]
+            row_out[side, r] = row.astype(jnp.bfloat16)
+
+    line = lax.broadcasted_iota(jnp.int32, (16, breadth), 0)
+    column = lax.broadcasted_iota(jnp.int32, (16, breadth), 1)
+    wanted = jnp.where(line < 2, breadth - 2 + line, line - 2)
+    chosen = jnp.where((column == wanted) & (line < 4), 1.0, 0.0).astype(jnp.bfloat16)
+    fill = jnp.zeros((LANES - fields, breadth), jnp.float32)
+
+    def pick(i, carry):
+        block = jnp.concatenate([wide[pl.ds(i, fields, stride=height), :], fill], axis=0)
+        picked = lax.dot_general(
+            chosen,
+            block.astype(jnp.bfloat16),
+            (((1,), (1,)), ((), ())),
+            preferred_element_type=jnp.float32,
+        )
+        edges[pl.ds(pl.multiple_of(i * 8, 8), 8), :] = picked[:8]
+        return carry
+
+    lax.fori_loop(0, height, pick, 0, unroll=8)
+    for side in range(2):
+        for q in range(2):
+            col = edges[pl.ds(2 * side + q, height, stride=8), :]
+            col_out[side, q] = col.astype(jnp.bfloat16)
+
+    pl.semaphore_wait(barrier, 4)
+    copies = []
+    for n in range(4):
+        source, target = (row_out, row_in) if n < 2 else (col_out, col_in)
+        copies.append(
+            pltpu.make_async_remote_copy(
+                src_ref=source.at[n % 2],
+                dst_ref=target.at[n % 2],
+                send_sem=sent.at[n],
+                recv_sem=came.at[n],
+                device_id=neighbour(n),
+                device_id_type=pl.DeviceIdType.MESH,
+            )
+        )
+        copies[-1].start()
+    for copy in copies:
+        copy.wait()
+    panel = lax.axis_index("panel")
+    zero = jnp.zeros(above.shape, jnp.bfloat16)
+    above[...] = jnp.where(panel > 0, row_in[0], zero)
+    below[...] = jnp.where(panel < lax.axis_size("panel") - 1, row_in[1], zero)
+    before[...] = col_in[0]
+    after[...] = col_in[1]
 
 
 def gather_kernel(
@@ -195,24 +270,30 @@
     ocean_cells = target_area.shape[0]
     pitch = breadth + 2 * LEFT
 
-    panels = lax.axis_size("panel")
-    columns = lax.axis_size("blk")
-    up = [(i, i + 1) for i in range(panels - 1)]
-    down = [(i + 1, i) for i in range(panels - 1)]
-    east = [(i, (i + 1) % columns) for i in range(columns)]
-    west = [(j, i) for i, j in east]
-    first_rows = jnp.transpose(source_flux[:, :2, :], (1, 0, 2))
-    last_rows = jnp.transpose(source_flux[:, height - 2 :, :], (1, 0, 2))
-    first_cols = jnp.transpose(source_flux[:, :, :2], (2, 1, 0))
-    last_cols = jnp.transpose(source_flux[:, :, breadth - 2 :], (2, 1, 0))
-    wide_lanes = ((0, 0), (0, 0), (0, LANES - fields))
-    above = lax.ppermute(last_rows, "panel", up)
-    below = lax.ppermute(first_rows, "panel", down)
-    before = lax.ppermute(jnp.pad(last_cols, wide_lanes), "blk", east)
-    after = lax.ppermute(jnp.pad(first_cols, wide_lanes), "blk", west)
-
     vmem = pl.BlockSpec(memory_space=pltpu.VMEM)
     smem = pl.BlockSpec(memory_space=pltpu.SMEM)
+    row_halo = jax.ShapeDtypeStruct((2, fields, breadth), jnp.bfloat16)
+    col_halo = jax.ShapeDtypeStruct((2, height, LANES), jnp.bfloat16)
+    above, below, before, after = pl.pallas_call(
+        halo_kernel,
+        out_shape=[row_halo, row_halo, col_halo, col_halo],
+        in_specs=[vmem],
+        out_specs=[vmem] * 4,
+        scratch_shapes=[
+            pltpu.VMEM((fields * height, breadth), jnp.float32),
+            pltpu.VMEM((height * 8, LANES), jnp.float32),
+            pltpu.VMEM((2, 2, fields, breadth), jnp.bfloat16),
+            pltpu.VMEM((2, 2, height, LANES), jnp.bfloat16),
+            pltpu.VMEM((2, 2, fields, breadth), jnp.bfloat16),
+            pltpu.VMEM((2, 2, height, LANES), jnp.bfloat16),
+            pltpu.SemaphoreType.DMA((4,)),
+            pltpu.SemaphoreType.DMA((4,)),
+        ],
+        compiler_params=pltpu.CompilerParams(
+            vmem_limit_bytes=48 * 2**20, collective_id=1, has_side_effects=True
+        ),
+        name="exchange_halos",
+    )(source_flux)
     records = pl.pallas_call(
         gather_kernel,
         out_shape=jax.ShapeDtypeStruct((members, fields, capacity), jnp.bfloat16),

time: 56.2 us -> 45 us (0.80)
  the two profiles are of different devices: /device:TPU:30 before, /device:TPU:0 now
where the time goes in v1:
time: 45 us; the launch traced here: 44.3 us
  Pallas kernels  42.1 us (94%)
  local copies, waits for them, and re-layouts  2.13 us (5%)
    pallas_call x1, Pallas kernels, on_device(): pl.pallas_call(gather_kernel, out_shape=jax.ShapeDtypeStruct((members, fi...  18.3 us
    pallas_call x1, Pallas kernels, on_device(): pl.pallas_call(scatter_kernel, out_shape=jax.ShapeDtypeStruct((fields, oc...  13.2 us
    pallas_call x1, Pallas kernels, on_device(): pl.pallas_call(halo_kernel, out_shape=[row_halo, row_halo, col_halo, col_...  10.6 us
    unnamed x17, local copies, waits for them, and re-layouts  2.13 us

profile of v1, /device:TPU:0, one launch (start us, length us, event | category | flops | bytes accessed | tf_op | source)
XLA Modules:
  0.0 44.3 jit_solution(115223337095435107)
XLA Ops:
  0.0 0.0 copy-start.7
  0.0 0.0 copy-start
  0.0 1.3 %copy-done = bf16[72,64,128]{2,1,0:T(8,128)(2,1)S(1)} copy-done((bf16[72,64,128]{2,1,0:T(8,128)(2,1)S(1)}, bf16[72,64,128]{2,1,0:T(8,128)(2,1)}, u32[]{:S(2)}) %copy-start) | copy-done | bytes 1179672
  1.3 0.0 copy-start.1
  1.3 0.0 copy-start.2
  1.3 0.0 copy-start.3
  1.3 0.0 copy-start.6
  1.3 10.6 %exchange_halos.1 = (bf16[2,72,128]{2,1,0:T(8,128)(2,1)S(1)}, bf16[2,72,128]{2,1,0:T(8,128)(2,1)S(1)}, bf16[2,64,128]{2,1,0:T(8,128)(2,1)S(1)}, bf16[2,64,128]{2,1,0:T(8,128)(2,1)S(1)}) custom-call(bf16[72,64,128]{2,1,0:T(8,128)(2,1)S(1)} %copy-done), custom_call_target="tpu_custom_call" | custom-call | tf_op jit(solution)/shard_map/exchange_halos/pallas_call | solution.py:277
  11.9 0.0 copy-start.4
  11.9 0.0 copy-start.5
  11.9 0.0 copy-done.7
  11.9 0.0 copy-done.1
  11.9 0.0 copy-done.2
  11.9 0.0 copy-done.3
  11.9 0.0 copy-done.6
  12.0 18.3 %gather_records.1.records = bf16[8,72,512]{2,1,0:T(8,128)(2,1)S(1)} custom-call(s32[8]{0:T(128)S(1)} %copy-done.7, s32[8,512]{1,0:T(8,128)S(1)} %copy-done.3, bf16[72,64,128]{2,1,0:T(8,128)(2,1)S(1)} %copy-done, bf16[2,72,128]{2,1,0:T(8,128)(2,1)S(1)} %get-tuple-element.9.above, bf16[2,72,128]{2,1,0:T(8,128)(2,1)S(1)} %get-tuple-element.10.below, ...), custom_call_target="tpu_custom_call" | custom-call | tf_op jit(solution)/shard_map/gather_records/pallas_call | solution.py:297
  30.2 0.0 copy-done.4
  30.3 0.0 copy-done.5
  30.3 13.2 %scatter_records.1 = bf16[72,4096]{1,0:T(8,128)(2,1)S(1)} custom-call(bf16[8,72,512]{2,1,0:T(8,128)(2,1)S(1)} %gather_records.1.records, s32[8,512]{1,0:T(8,128)S(1)} %copy-done.4, f32[1,4096]{1,0:T(1,128)S(1)} %bitcast.1), custom_call_target="tpu_custom_call" | custom-call | tf_op jit(solution)/shard_map/scatter_records/pallas_call | solution.py:323
  43.5 0.8 %copy.10 = bf16[72,4096]{1,0:T(8,128)(2,1)} copy(bf16[72,4096]{1,0:T(8,128)(2,1)S(1)} %scatter_records.1) | data formatting | bytes 1179648
Async XLA Ops:
  0.0 11.9 %copy-start.7 = (s32[8]{0:T(128)S(1)}, s32[8]{0:T(128)}, u32[]{:S(2)}) copy-start(s32[8]{0:T(128)} %count.1) | copy-start | bytes 100
  0.0 1.3 %copy-start = (bf16[72,64,128]{2,1,0:T(8,128)(2,1)S(1)}, bf16[72,64,128]{2,1,0:T(8,128)(2,1)}, u32[]{:S(2)}) copy-start(bf16[72,64,128]{2,1,0:T(8,128)(2,1)} %flux.3) | copy-start | bytes 3538948
  1.3 10.6 %copy-start.1 = (f32[2,4,8,512]{3,2,1,0:T(8,128)S(1)}, f32[2,4,8,512]{3,2,1,0:T(8,128)}, u32[]{:S(2)}) copy-start(f32[2,4,8,512]{3,2,1,0:T(8,128)} %offset.1) | copy-start | bytes 393220
  1.3 10.6 %copy-start.2 = (f32[4,8,512]{2,1,0:T(8,128)S(1)}, f32[4,8,512]{2,1,0:T(8,128)}, u32[]{:S(2)}) copy-start(f32[4,8,512]{2,1,0:T(8,128)} %weight.1) | copy-start | bytes 196612
  1.3 10.6 %copy-start.3 = (s32[8,512]{1,0:T(8,128)S(1)}, s32[8,512]{1,0:T(8,128)}, u32[]{:S(2)}) copy-start(s32[8,512]{1,0:T(8,128)} %cells.1) | copy-start | bytes 49156
  1.3 10.7 %copy-start.6 = (bf16[24,256]{1,0:T(8,128)(2,1)S(1)}, bf16[24,256]{1,0:T(8,128)(2,1)}, u32[]{:S(2)}) copy-start(bf16[24,256]{1,0:T(8,128)(2,1)} %constant.2.clone.pattern) | copy-start | bytes 36868
  11.9 18.4 %copy-start.4 = (s32[8,512]{1,0:T(8,128)S(1)}, s32[8,512]{1,0:T(8,128)}, u32[]{:S(2)}) copy-start(s32[8,512]{1,0:T(8,128)} %target.1) | copy-start | bytes 49156
  11.9 18.4 %copy-start.5 = (f32[4096]{0:T(1024)S(1)}, f32[4096]{0:T(1024)}, u32[]{:S(2)}) copy-start(f32[4096]{0:T(1024)} %param.14) | copy-start | bytes 49156

commit v2 on v0

v2 whole, which is shorter than its diff:
```python
import jax
import jax.numpy as jnp
import numpy as np
from jax import lax
from jax.experimental import pallas as pl
from jax.experimental.pallas import tpu as pltpu
from jax.sharding import PartitionSpec as P

LANES = 128
GROUP = 16
TAPS = 16
LEFT = 8
PARTS = 3
LAG = 3
PAIR = 2
LOW = 256


def tap_pattern():
    first = np.array([1, -8, 0, 8, -1, 0, 0, 0])
    second = np.array([-1, 16, -30, 16, -1, 0, 0, 0])
    here = np.array([0, 0, 1, 0, 0, 0, 0, 0])
    none = np.zeros(8)
    rows = [
        np.concatenate([here, none]),
        np.concatenate([none, first]),
        np.concatenate([first, none]),
        np.concatenate([none, second]),
        np.concatenate([second, none]),
    ]
    rows += [np.zeros(TAPS)] * 3
    return np.tile(np.stack(rows), (PARTS, GROUP)).astype(np.float32)


def remap_kernel(
    count, cells, flux, weight, offset, pattern, targets, area, out,
    wide, grid, edges, mom, row_out, col_out, row_in, col_in, records, landed, masked, total,
    halo_sent, halo_came, sent, came,
):
    fields, height, breadth = flux.shape
    members, capacity = cells.shape
    pitch = breadth + 2 * LEFT
    chunks = capacity // LANES
    shift = breadth.bit_length() - 1
    assert breadth == 1 << shift
    digits = out.shape[1] // LOW
    rows = total.shape[0] // digits
    axes = ("panel", "panel", "blk", "blk")
    shifts = (1, -1, 1, -1)
    mesh_id = pl.DeviceIdType.MESH
    me = lax.axis_index("blk")

    def neighbour(n):
        size = lax.axis_size(axes[n])
        return {axes[n]: lax.rem(lax.axis_index(axes[n]) + shifts[n] + size, size)}

    def member(step):
        return lax.rem(me + step, members)

    barrier = pltpu.get_barrier_semaphore()
    for n in range(2):
        pl.semaphore_signal(barrier, 1, device_id=neighbour(n), device_id_type=mesh_id)
    for step in range(1, members):
        pl.semaphore_signal(barrier, 1, device_id={"blk": member(step)}, device_id_type=mesh_id)

    def widen(f, carry):
        wide[pl.ds(f * height, height), :] = flux[f].astype(jnp.float32)
        return carry

    lax.fori_loop(0, fields, widen, 0, unroll=8)
    for side, first in enumerate((height - 2, 0)):
        for r in range(2):
            row = wide[pl.ds(first + r, fields, stride=height), :]
            row_out[side, r] = row.astype(jnp.bfloat16)

    line = lax.broadcasted_iota(jnp.int32, (16, breadth), 0)
    column = lax.broadcasted_iota(jnp.int32, (16, breadth), 1)
    wanted = jnp.where(line < 2, breadth - 2 + line, line - 2)
    chosen = jnp.where((column == wanted) & (line < 4), 1.0, 0.0).astype(jnp.bfloat16)
    fill = jnp.zeros((LANES - fields, breadth), jnp.float32)

    def pick(i, carry):
        block = jnp.concatenate([wide[pl.ds(i, fields, stride=height), :], fill], axis=0)
        picked = lax.dot_general(
            chosen,
            block.astype(jnp.bfloat16),
            (((1,), (1,)), ((), ())),
            preferred_element_type=jnp.float32,
        )
        edges[pl.ds(pl.multiple_of(i * 8, 8), 8), :] = picked[:8]
        return carry

    lax.fori_loop(0, height, pick, 0, unroll=8)
    for side in range(2):
        for q in range(2):
            col = edges[pl.ds(2 * side + q, height, stride=8), :]
            col_out[side, q] = col.astype(jnp.bfloat16)

    pl.semaphore_wait(barrier, members + 1)
    halos = []
    for n in range(4):
        source, target = (row_out, row_in) if n < 2 else (col_out, col_in)
        halos.append(
            pltpu.make_async_remote_copy(
                src_ref=source.at[n % 2],
                dst_ref=target.at[n % 2],
                send_sem=halo_sent.at[n],
                recv_sem=halo_came.at[n],
                device_id=neighbour(n),
                device_id_type=mesh_id,
            )
        )
        halos[-1].start()

    total[...] = jnp.zeros_like(total)
    gap = jnp.zeros((LEFT, LANES), jnp.float32)
    grid[(height + 4) * pitch :, :] = jnp.zeros((4 * pitch, LANES), jnp.float32)

    def place(row, block):
        start = pl.multiple_of(row * pitch, 8)
        turned = jnp.concatenate([block, fill], axis=0).T
        grid[pl.ds(start, LEFT), :] = gap
        grid[pl.ds(start + LEFT, breadth), :] = turned
        grid[pl.ds(start + LEFT + breadth, LEFT), :] = gap

    def turn(i, carry):
        place(i + 2, wide[pl.ds(i, fields, stride=height), :])
        return carry

    lax.fori_loop(0, height, turn, 0, unroll=4)

    w = weight[...]
    ox = offset[0]
    oy = offset[1]
    moments = [
        jnp.sum(w, axis=0),
        jnp.sum(w * ox, axis=0) / 12.0,
        jnp.sum(w * oy, axis=0) / 12.0,
        0.5 * jnp.sum(w * ox * ox, axis=0) / 12.0,
        0.5 * jnp.sum(w * oy * oy, axis=0) / 12.0,
    ]
    mom[...] = jnp.zeros_like(mom)
    slots = lax.broadcasted_iota(jnp.int32, (1, capacity), 1)
    alive = [slots < count[k] for k in range(members)]
    for m, moment in enumerate(moments):
        for part in range(PARTS):
            piece = moment.astype(jnp.bfloat16).astype(jnp.float32)
            moment = moment - piece
            for k in range(members):
                mom[k, part * 8 + m : part * 8 + m + 1, :] = jnp.where(
                    alive[k], piece[k : k + 1, :], 0.0
                )

    for halo in halos:
        halo.wait()
    panel = lax.axis_index("panel")
    has_above = jnp.where(panel > 0, 1.0, 0.0)
    has_below = jnp.where(panel < lax.axis_size("panel") - 1, 1.0, 0.0)
    for r in range(2):
        place(r, row_in[0, r].astype(jnp.float32) * has_above)
        place(height + 2 + r, row_in[1, r].astype(jnp.float32) * has_below)
    for q in range(2):
        grid[pl.ds(2 * pitch + LEFT - 2 + q, height, stride=pitch), :] = col_in[0, q].astype(
            jnp.float32
        )
        grid[pl.ds(2 * pitch + LEFT + breadth + q, height, stride=pitch), :] = col_in[1, q].astype(
            jnp.float32
        )

    slot_group = lax.broadcasted_iota(jnp.int32, (LANES, GROUP * TAPS), 0) % GROUP
    tap_group = lax.broadcasted_iota(jnp.int32, (LANES, GROUP * TAPS), 1) // TAPS
    diagonal = slot_group == tap_group

    def gather(k, step, start):
        m = mom[k, :, pl.ds(start, LANES)].T.astype(jnp.bfloat16)
        coef = jnp.dot(m, pattern[...], preferred_element_type=jnp.float32)
        coef = jnp.where(diagonal, coef, 0.0)
        high = coef.astype(jnp.bfloat16)
        low = (coef - high.astype(jnp.float32)).astype(jnp.bfloat16)
        parts = []
        for g in range(LANES // GROUP):
            taps = []
            for s in range(GROUP):
                cell = cells[k, start + g * GROUP + s]
                base = cell + lax.shift_right_logical(cell, shift) * (pitch - breadth)
                taps.append(grid[pl.ds(base + 2 * pitch + LEFT - 2, 8), :])
                taps.append(grid[pl.ds(base + LEFT, 8, stride=pitch), :])
            picked = jnp.concatenate(taps, axis=0).astype(jnp.bfloat16)
            some = slice(g * GROUP, (g + 1) * GROUP)
            both = jnp.concatenate([high[some], low[some]], axis=0)
            r = jnp.dot(both, picked, preferred_element_type=jnp.float32)
            parts.append(r[:GROUP] + r[GROUP:])
        record = jnp.concatenate(parts, axis=0).T
        records[step - 1, :, pl.ds(start, LANES)] = record[:fields].astype(jnp.bfloat16)

    def send(step):
        return pltpu.make_async_remote_copy(
            src_ref=records.at[step - 1],
            dst_ref=landed.at[step - 1],
            send_sem=sent.at[step - 1],
            recv_sem=came.at[step - 1],
            device_id={"blk": member(step)},
            device_id_type=mesh_id,
        )

    rest = jnp.zeros((rows - fields, capacity), jnp.bfloat16)

    def deposit(record, source):
        cell = targets[pl.ds(source, 1), :]
        high = lax.shift_right_logical(cell, LOW.bit_length() - 1)
        low = cell & (LOW - 1)
        spots = lax.broadcasted_iota(jnp.int32, (LOW, capacity), 0)
        table = jnp.where(spots == low, 1.0, 0.0).astype(jnp.bfloat16)
        record = jnp.concatenate([record, rest], axis=0)
        for h in range(digits):
            here = jnp.where(high == h, 1.0, 0.0).astype(jnp.bfloat16)
            masked[h * rows : (h + 1) * rows, :] = record * here
        total[...] += lax.dot_general(
            masked[...], table, (((1,), (1,)), ((), ())), preferred_element_type=jnp.float32
        )

    def arrival(step, carry):
        send(step).wait_recv()
        deposit(landed[step - 1], lax.rem(me - step + members, members))
        return carry

    def advance(step, carry):
        def pair(p, inner):
            for c in range(PAIR):
                gather(member(step), step, pl.multiple_of((p * PAIR + c) * LANES, LANES))
            return inner

        lax.fori_loop(0, chunks // PAIR, pair, 0)

        @pl.when(step < members)
        def _():
            send(step).start()

        @pl.when(step > LAG)
        def _():
            arrival(step - LAG, 0)

        return carry

    lax.fori_loop(1, members + 1, advance, 0)
    deposit(records[members - 1], me)
    lax.fori_loop(members + 1 - LAG, members, arrival, 0)
    for h in range(digits):
        columns = slice(h * LOW, (h + 1) * LOW)
        value = total[h * rows : h * rows + fields, :] / area[:, columns]
        out[:, columns] = value.astype(jnp.bfloat16)

    def finish(step, carry):
        send(step).wait_send()
        return carry

    lax.fori_loop(1, members, finish, 0)


def on_device(
    source_flux, gauss_weight, gauss_offset, slot_count, source_cell, target_cell, target_area
):
    fields, height, breadth = source_flux.shape
    members, capacity = source_cell.shape
    ocean_cells = target_area.shape[0]
    pitch = breadth + 2 * LEFT
    digits = ocean_cells // LOW
    rows = -(-fields // 16) * 16
    vmem = pl.BlockSpec(memory_space=pltpu.VMEM)
    smem = pl.BlockSpec(memory_space=pltpu.SMEM)
    return pl.pallas_call(
        remap_kernel,
        out_shape=jax.ShapeDtypeStruct((fields, ocean_cells), jnp.bfloat16),
        in_specs=[smem, smem] + [vmem] * 6,
        out_specs=vmem,
        scratch_shapes=[
            pltpu.VMEM((fields * height, breadth), jnp.float32),
            pltpu.VMEM(((height + 8) * pitch, LANES), jnp.float32),
            pltpu.VMEM((height * 8, LANES), jnp.float32),
            pltpu.VMEM((members, 8 * PARTS, capacity), jnp.float32),
            pltpu.VMEM((2, 2, fields, breadth), jnp.bfloat16),
            pltpu.VMEM((2, 2, height, LANES), jnp.bfloat16),
            pltpu.VMEM((2, 2, fields, breadth), jnp.bfloat16),
            pltpu.VMEM((2, 2, height, LANES), jnp.bfloat16),
            pltpu.VMEM((members, fields, capacity), jnp.bfloat16),
            pltpu.VMEM((members - 1, fields, capacity), jnp.bfloat16),
            pltpu.VMEM((digits * rows, capacity), jnp.bfloat16),
            pltpu.VMEM((digits * rows, LOW), jnp.float32),
            pltpu.SemaphoreType.DMA((4,)),
            pltpu.SemaphoreType.DMA((4,)),
            pltpu.SemaphoreType.DMA((members - 1,)),
            pltpu.SemaphoreType.DMA((members - 1,)),
        ],
        compiler_params=pltpu.CompilerParams(
            vmem_limit_bytes=48 * 2**20, collective_id=0, has_side_effects=True
        ),
        name="remap",
    )(
        slot_count,
        source_cell,
        source_flux,
        gauss_weight,
        gauss_offset,
        jnp.asarray(tap_pattern(), jnp.bfloat16),
        target_cell,
        target_area.reshape(1, ocean_cells),
    )


def solution(mesh):
    placed = (
        P(None, "panel", "blk"),
        P(None, ("panel", "blk"), None),
        P(None, None, ("panel", "blk"), None),
        P(("panel", "blk")),
        P(("panel", "blk"), None),
        P(("panel", "blk"), None),
        P(("panel", "blk")),
    )
    return jax.shard_map(
        on_device, mesh=mesh, in_specs=placed, out_specs=P(None, ("panel", "blk")), check_vma=False
    )
```

time: 56.2 us -> 41.4 us (0.74)
  the two profiles are of different devices: /device:TPU:30 before, /device:TPU:0 now
where the time goes in v2:
time: 41.4 us; the launch traced here: 40.9 us
  Pallas kernels  33.6 us (81%)
  local copies, waits for them, and re-layouts  7.34 us (18%)
    pallas_call x1, Pallas kernels, on_device(): pl.pallas_call(remap_kernel, out_shape=jax.ShapeDtypeStruct((fields, ocea...  33.6 us
    unnamed x17, local copies, waits for them, and re-layouts  7.34 us

profile of v2, /device:TPU:0, one launch (start us, length us, event | category | flops | bytes accessed | tf_op | source)
XLA Modules:
  0.0 40.9 jit_solution(14261991335216738204)
XLA Ops:
  0.0 0.0 copy-start
  0.0 1.3 %copy-done = bf16[72,64,128]{2,1,0:T(8,128)(2,1)S(1)} copy-done((bf16[72,64,128]{2,1,0:T(8,128)(2,1)S(1)}, bf16[72,64,128]{2,1,0:T(8,128)(2,1)}, u32[]{:S(2)}) %copy-start) | copy-done | bytes 1179672
  1.3 0.0 copy-start.1
  1.3 0.9 %copy-done.1 = f32[2,4,8,512]{3,2,1,0:T(8,128)S(1)} copy-done((f32[2,4,8,512]{3,2,1,0:T(8,128)S(1)}, f32[2,4,8,512]{3,2,1,0:T(8,128)}, u32[]{:S(2)}) %copy-start.1) | copy-done | bytes 131096
  2.2 0.0 copy-start.2
  2.2 0.8 %copy-done.2 = f32[4,8,512]{2,1,0:T(8,128)S(1)} copy-done((f32[4,8,512]{2,1,0:T(8,128)S(1)}, f32[4,8,512]{2,1,0:T(8,128)}, u32[]{:S(2)}) %copy-start.2) | copy-done | bytes 65560
  3.0 0.0 copy-start.3
  3.0 0.7 %copy-done.3 = s32[8,512]{1,0:T(8,128)S(1)} copy-done((s32[8,512]{1,0:T(8,128)S(1)}, s32[8,512]{1,0:T(8,128)}, u32[]{:S(2)}) %copy-start.3) | copy-done | bytes 16408
  3.7 0.0 copy-start.4
  3.7 0.7 %copy-done.4 = s32[8,512]{1,0:T(8,128)S(1)} copy-done((s32[8,512]{1,0:T(8,128)S(1)}, s32[8,512]{1,0:T(8,128)}, u32[]{:S(2)}) %copy-start.4) | copy-done | bytes 16408
  4.5 0.0 copy-start.5
  4.5 0.7 %copy-done.5 = f32[4096]{0:T(1024)S(1)} copy-done((f32[4096]{0:T(1024)S(1)}, f32[4096]{0:T(1024)}, u32[]{:S(2)}) %copy-start.5) | copy-done | bytes 16408
  5.2 0.0 copy-start.6
  5.2 0.7 %copy-done.6 = bf16[24,256]{1,0:T(8,128)(2,1)S(1)} copy-done((bf16[24,256]{1,0:T(8,128)(2,1)S(1)}, bf16[24,256]{1,0:T(8,128)(2,1)}, u32[]{:S(2)}) %copy-start.6) | copy-done | bytes 12312
  5.9 0.0 copy-start.7
  5.9 0.7 %copy-done.7 = s32[8]{0:T(128)S(1)} copy-done((s32[8]{0:T(128)S(1)}, s32[8]{0:T(128)}, u32[]{:S(2)}) %copy-start.7) | copy-done | bytes 56
  6.5 33.6 %remap.1 = bf16[72,4096]{1,0:T(8,128)(2,1)S(1)} custom-call(s32[8]{0:T(128)S(1)} %copy-done.7, s32[8,512]{1,0:T(8,128)S(1)} %copy-done.3, bf16[72,64,128]{2,1,0:T(8,128)(2,1)S(1)} %copy-done, f32[4,8,512]{2,1,0:T(8,128)S(1)} %copy-done.2, f32[2,4,8,512]{3,2,1,0:T(8,128)S(1)} %copy-done.1, bf16[24,256]{1,0:T(8,128)(2,1)S(1)} %copy-done.6, ...), custom_call_target="tpu_custom_call" | custom-call | tf_op jit(solution)/shard_map/remap/pallas_call | solution.py:271
  40.1 0.8 %copy.10 = bf16[72,4096]{1,0:T(8,128)(2,1)} copy(bf16[72,4096]{1,0:T(8,128)(2,1)S(1)} %remap.1) | data formatting | bytes 1179648
Async XLA Ops:
  0.0 1.3 %copy-start = (bf16[72,64,128]{2,1,0:T(8,128)(2,1)S(1)}, bf16[72,64,128]{2,1,0:T(8,128)(2,1)}, u32[]{:S(2)}) copy-start(bf16[72,64,128]{2,1,0:T(8,128)(2,1)} %flux.1) | copy-start | bytes 3538948
  1.3 0.9 %copy-start.1 = (f32[2,4,8,512]{3,2,1,0:T(8,128)S(1)}, f32[2,4,8,512]{3,2,1,0:T(8,128)}, u32[]{:S(2)}) copy-start(f32[2,4,8,512]{3,2,1,0:T(8,128)} %offset.1) | copy-start | bytes 393220
  2.2 0.8 %copy-start.2 = (f32[4,8,512]{2,1,0:T(8,128)S(1)}, f32[4,8,512]{2,1,0:T(8,128)}, u32[]{:S(2)}) copy-start(f32[4,8,512]{2,1,0:T(8,128)} %weight.1) | copy-start | bytes 196612
  3.0 0.7 %copy-start.3 = (s32[8,512]{1,0:T(8,128)S(1)}, s32[8,512]{1,0:T(8,128)}, u32[]{:S(2)}) copy-start(s32[8,512]{1,0:T(8,128)} %cells.1) | copy-start | bytes 49156
  3.7 0.7 %copy-start.4 = (s32[8,512]{1,0:T(8,128)S(1)}, s32[8,512]{1,0:T(8,128)}, u32[]{:S(2)}) copy-start(s32[8,512]{1,0:T(8,128)} %targets.1) | copy-start | bytes 49156
  4.5 0.7 %copy-start.5 = (f32[4096]{0:T(1024)S(1)}, f32[4096]{0:T(1024)}, u32[]{:S(2)}) copy-start(f32[4096]{0:T(1024)} %param.14) | copy-start | bytes 49156
  5.2 0.7 %copy-start.6 = (bf16[24,256]{1,0:T(8,128)(2,1)S(1)}, bf16[24,256]{1,0:T(8,128)(2,1)}, u32[]{:S(2)}) copy-start(bf16[24,256]{1,0:T(8,128)(2,1)} %constant.2.clone.pattern) | copy-start | bytes 36868
  5.9 0.7 %copy-start.7 = (s32[8]{0:T(128)S(1)}, s32[8]{0:T(128)}, u32[]{:S(2)}) copy-start(s32[8]{0:T(128)} %count.1) | copy-start | bytes 100

commit v3 on v2

--- a/solution.py
+++ b/solution.py
@@ -33,13 +33,14 @@
 
 
 def remap_kernel(
-    count, cells, flux, weight, offset, pattern, targets, area, out,
-    wide, grid, edges, mom, row_out, col_out, row_in, col_in, records, landed, masked, total,
+    count, hbm_cells, hbm_flux, hbm_weight, hbm_offset, hbm_pattern, hbm_targets, hbm_area, out,
+    cells, flux, weight, offset, pattern, targets, area, loaded, wide, grid, edges, mom, row_out, col_out, row_in, col_in, records, landed, masked, total,
     halo_sent, halo_came, sent, came,
 ):
     fields, height, breadth = flux.shape
     members, capacity = cells.shape
-    pitch = breadth + 2 * LEFT
+    pitch = breadth + 2 * LEFT + 1
+    deep = height + 1
     chunks = capacity // LANES
     shift = breadth.bit_length() - 1
     assert breadth == 1 << shift
@@ -57,6 +58,22 @@
     def member(step):
         return lax.rem(me + step, members)
 
+    loads = [
+        pltpu.make_async_copy(source, target, loaded.at[n])
+        for n, (source, target) in enumerate(
+            (
+                (hbm_flux, flux),
+                (hbm_weight, weight),
+                (hbm_offset, offset),
+                (hbm_pattern, pattern),
+                (hbm_cells, cells),
+                (hbm_targets, targets),
+                (hbm_area, area),
+            )
+        )
+    ]
+    for load in loads:
+        load.start()
     barrier = pltpu.get_barrier_semaphore()
     for n in range(2):
         pl.semaphore_signal(barrier, 1, device_id=neighbour(n), device_id_type=mesh_id)
@@ -64,13 +81,14 @@
         pl.semaphore_signal(barrier, 1, device_id={"blk": member(step)}, device_id_type=mesh_id)
 
     def widen(f, carry):
-        wide[pl.ds(f * height, height), :] = flux[f].astype(jnp.float32)
-        return carry
-
+        wide[pl.ds(f * deep, height), :] = flux[f].astype(jnp.float32)
+        return carry
+
+    loads[0].wait()
     lax.fori_loop(0, fields, widen, 0, unroll=8)
     for side, first in enumerate((height - 2, 0)):
         for r in range(2):
-            row = wide[pl.ds(first + r, fields, stride=height), :]
+            row = wide[pl.ds(first + r, fields, stride=deep), :]
             row_out[side, r] = row.astype(jnp.bfloat16)
 
     line = lax.broadcasted_iota(jnp.int32, (16, breadth), 0)
@@ -80,7 +98,7 @@
     fill = jnp.zeros((LANES - fields, breadth), jnp.float32)
 
     def pick(i, carry):
-        block = jnp.concatenate([wide[pl.ds(i, fields, stride=height), :], fill], axis=0)
+        block = jnp.concatenate([wide[pl.ds(i, fields, stride=deep), :], fill], axis=0)
         picked = lax.dot_general(
             chosen,
             block.astype(jnp.bfloat16),
@@ -117,18 +135,20 @@
     grid[(height + 4) * pitch :, :] = jnp.zeros((4 * pitch, LANES), jnp.float32)
 
     def place(row, block):
-        start = pl.multiple_of(row * pitch, 8)
+        start = row * pitch
         turned = jnp.concatenate([block, fill], axis=0).T
         grid[pl.ds(start, LEFT), :] = gap
         grid[pl.ds(start + LEFT, breadth), :] = turned
         grid[pl.ds(start + LEFT + breadth, LEFT), :] = gap
 
     def turn(i, carry):
-        place(i + 2, wide[pl.ds(i, fields, stride=height), :])
+        place(i + 2, wide[pl.ds(i, fields, stride=deep), :])
         return carry
 
     lax.fori_loop(0, height, turn, 0, unroll=4)
 
+    for load in loads[1:]:
+        load.wait()
     w = weight[...]
     ox = offset[0]
     oy = offset[1]
@@ -263,18 +283,28 @@
     fields, height, breadth = source_flux.shape
     members, capacity = source_cell.shape
     ocean_cells = target_area.shape[0]
-    pitch = breadth + 2 * LEFT
+    pitch = breadth + 2 * LEFT + 1
     digits = ocean_cells // LOW
     rows = -(-fields // 16) * 16
     vmem = pl.BlockSpec(memory_space=pltpu.VMEM)
     smem = pl.BlockSpec(memory_space=pltpu.SMEM)
+    hbm = pl.BlockSpec(memory_space=pltpu.HBM)
+    pattern = jnp.asarray(tap_pattern(), jnp.bfloat16)
     return pl.pallas_call(
         remap_kernel,
         out_shape=jax.ShapeDtypeStruct((fields, ocean_cells), jnp.bfloat16),
-        in_specs=[smem, smem] + [vmem] * 6,
+        in_specs=[smem] + [hbm] * 7,
         out_specs=vmem,
         scratch_shapes=[
-            pltpu.VMEM((fields * height, breadth), jnp.float32),
+            pltpu.SMEM(source_cell.shape, jnp.int32),
+            pltpu.VMEM(source_flux.shape, jnp.bfloat16),
+            pltpu.VMEM(gauss_weight.shape, jnp.float32),
+            pltpu.VMEM(gauss_offset.shape, jnp.float32),
+            pltpu.VMEM(pattern.shape, jnp.bfloat16),
+            pltpu.VMEM(target_cell.shape, jnp.int32),
+            pltpu.VMEM((1, ocean_cells), jnp.float32),
+            pltpu.SemaphoreType.DMA((7,)),
+            pltpu.VMEM((fields * (height + 1), breadth), jnp.float32),
             pltpu.VMEM(((height + 8) * pitch, LANES), jnp.float32),
             pltpu.VMEM((height * 8, LANES), jnp.float32),
             pltpu.VMEM((members, 8 * PARTS, capacity), jnp.float32),
@@ -292,7 +322,7 @@
             pltpu.SemaphoreType.DMA((members - 1,)),
         ],
         compiler_params=pltpu.CompilerParams(
-            vmem_limit_bytes=48 * 2**20, collective_id=0, has_side_effects=True
+            vmem_limit_bytes=63 * 2**20, collective_id=0, has_side_effects=True
         ),
         name="remap",
     )(
@@ -301,7 +331,7 @@
         source_flux,
         gauss_weight,
         gauss_offset,
-        jnp.asarray(tap_pattern(), jnp.bfloat16),
+        pattern,
         target_cell,
         target_area.reshape(1, ocean_cells),
     )

time: 41.4 us -> 36.3 us (0.88)
  local copies, waits for them, and re-layouts: 7.34 us -> 1.92 us
  Pallas kernels: 33.6 us -> 34.2 us
    unnamed x17 -> x1, local copies, waits for them, and re-layouts: 7.34 us -> 1.92 us
    pallas_call x1, Pallas kernels: 33.6 us -> 34.2 us  [on_device(): pl.pallas_call(remap_kernel, out_shape=jax.ShapeDtypeStruct((fields, ocea...]
where the time goes in v3:
time: 36.3 us; the launch traced here: 36.1 us
  Pallas kernels  34.2 us (94%)
  local copies, waits for them, and re-layouts  1.92 us (5%)
    pallas_call x1, Pallas kernels, on_device(): pl.pallas_call(remap_kernel, out_shape=jax.ShapeDtypeStruct((fields, ocea...  34.2 us
    unnamed x1, local copies, waits for them, and re-layouts  1.92 us

profile of v3, /device:TPU:0, one launch (start us, length us, event | category | flops | bytes accessed | tf_op | source)
XLA Modules:
  0.0 36.1 jit_solution(1515694405397047116)
XLA Ops:
  0.0 34.2 %remap.1 = bf16[72,4096]{1,0:T(8,128)(2,1)} custom-call(s32[8]{0:T(128)} %count.1, s32[8,512]{1,0:T(8,128)} %hbm_cells.1, bf16[72,64,128]{2,1,0:T(8,128)(2,1)} %hbm_flux.1, f32[4,8,512]{2,1,0:T(8,128)} %hbm_weight.1, f32[2,4,8,512]{3,2,1,0:T(8,128)} %hbm_offset.1, bf16[24,256]{1,0:T(8,128)(2,1)} %constant.2.clone.hbm_pattern, s32[8,512]{1,0:T(8,128)} %hbm_targets.1, ...), custom_call_target="tpu_custom_call" | custom-call | tf_op jit(solution)/shard_map/remap/pallas_call | solution.py:293
  34.2 1.9 %copy.10 = bf16[72,4096]{1,0:T(8,128)(2,1)} copy(bf16[72,4096]{1,0:T(8,128)(2,1)} %remap.1) | data formatting | bytes 1179648

commit v4 on v3

--- a/solution.py
+++ b/solution.py
@@ -33,8 +33,8 @@
 
 
 def remap_kernel(
-    count, hbm_cells, hbm_flux, hbm_weight, hbm_offset, hbm_pattern, hbm_targets, hbm_area, out,
-    cells, flux, weight, offset, pattern, targets, area, loaded, wide, grid, edges, mom, row_out, col_out, row_in, col_in, records, landed, masked, total,
+    count, hbm_cells, hbm_flux, hbm_weight, hbm_offset, hbm_pattern, hbm_targets, out,
+    cells, bases, places, flux, weight, offset, pattern, targets, loaded, placed, wide, grid, edges, mom, row_out, col_out, row_in, col_in, records, landed, masked, total,
     halo_sent, halo_came, sent, came,
 ):
     fields, height, breadth = flux.shape
@@ -68,7 +68,6 @@
                 (hbm_pattern, pattern),
                 (hbm_cells, cells),
                 (hbm_targets, targets),
-                (hbm_area, area),
             )
         )
     ]
@@ -149,6 +148,10 @@
 
     for load in loads[1:]:
         load.wait()
+    cell = cells[...]
+    bases[...] = cell + lax.shift_right_logical(cell, shift) * (pitch - breadth)
+    placing = pltpu.make_async_copy(bases, places, placed)
+    placing.start()
     w = weight[...]
     ox = offset[0]
     oy = offset[1]
@@ -171,6 +174,7 @@
                     alive[k], piece[k : k + 1, :], 0.0
                 )
 
+    placing.wait()
     for halo in halos:
         halo.wait()
     panel = lax.axis_index("panel")
@@ -201,8 +205,7 @@
         for g in range(LANES // GROUP):
             taps = []
             for s in range(GROUP):
-                cell = cells[k, start + g * GROUP + s]
-                base = cell + lax.shift_right_logical(cell, shift) * (pitch - breadth)
+                base = places[k, start + g * GROUP + s]
                 taps.append(grid[pl.ds(base + 2 * pitch + LEFT - 2, 8), :])
                 taps.append(grid[pl.ds(base + LEFT, 8, stride=pitch), :])
             picked = jnp.concatenate(taps, axis=0).astype(jnp.bfloat16)
@@ -267,8 +270,7 @@
     lax.fori_loop(members + 1 - LAG, members, arrival, 0)
     for h in range(digits):
         columns = slice(h * LOW, (h + 1) * LOW)
-        value = total[h * rows : h * rows + fields, :] / area[:, columns]
-        out[:, columns] = value.astype(jnp.bfloat16)
+        out[:, columns] = total[h * rows : h * rows + fields, :]
 
     def finish(step, carry):
         send(step).wait_send()
@@ -290,20 +292,22 @@
     smem = pl.BlockSpec(memory_space=pltpu.SMEM)
     hbm = pl.BlockSpec(memory_space=pltpu.HBM)
     pattern = jnp.asarray(tap_pattern(), jnp.bfloat16)
-    return pl.pallas_call(
+    integrated = pl.pallas_call(
         remap_kernel,
-        out_shape=jax.ShapeDtypeStruct((fields, ocean_cells), jnp.bfloat16),
-        in_specs=[smem] + [hbm] * 7,
+        out_shape=jax.ShapeDtypeStruct((fields, ocean_cells), jnp.float32),
+        in_specs=[smem] + [hbm] * 6,
         out_specs=vmem,
         scratch_shapes=[
+            pltpu.VMEM(source_cell.shape, jnp.int32),
+            pltpu.VMEM(source_cell.shape, jnp.int32),
             pltpu.SMEM(source_cell.shape, jnp.int32),
             pltpu.VMEM(source_flux.shape, jnp.bfloat16),
             pltpu.VMEM(gauss_weight.shape, jnp.float32),
             pltpu.VMEM(gauss_offset.shape, jnp.float32),
             pltpu.VMEM(pattern.shape, jnp.bfloat16),
             pltpu.VMEM(target_cell.shape, jnp.int32),
-            pltpu.VMEM((1, ocean_cells), jnp.float32),
-            pltpu.SemaphoreType.DMA((7,)),
+            pltpu.SemaphoreType.DMA((6,)),
+            pltpu.SemaphoreType.DMA,
             pltpu.VMEM((fields * (height + 1), breadth), jnp.float32),
             pltpu.VMEM(((height + 8) * pitch, LANES), jnp.float32),
             pltpu.VMEM((height * 8, LANES), jnp.float32),
@@ -333,8 +337,8 @@
         gauss_offset,
         pattern,
         target_cell,
-        target_area.reshape(1, ocean_cells),
     )
+    return (integrated / target_area[None, :]).astype(jnp.bfloat16)
 
 
 def solution(mesh):

time: 36.3 us -> 35.1 us (0.967)
  other arithmetic: 0 us -> 2.17 us
  local copies, waits for them, and re-layouts: 1.92 us -> 0.01 us
  Pallas kernels: 34.2 us -> 32.6 us
    convert_element_type x0 -> x1, other arithmetic: none -> 2.17 us  [on_device(): return (integrated / target_area[None, :]).astype(jnp.bfloat16)]
    unnamed x1 -> x2, local copies, waits for them, and re-layouts: 1.92 us -> 0.01 us
    pallas_call x1, Pallas kernels: 34.2 us -> 32.6 us  [on_device(): pl.pallas_call(remap_kernel, out_shape=jax.ShapeDtypeStruct((fields, ocea...]
where the time goes in v4:
time: 35.1 us; the launch traced here: 34.8 us
  Pallas kernels  32.6 us (93%)
  other arithmetic  2.17 us (6%)
    pallas_call x1, Pallas kernels, on_device(): pl.pallas_call(remap_kernel, out_shape=jax.ShapeDtypeStruct((fields, ocea...  32.6 us
    convert_element_type x1, other arithmetic, on_device(): return (integrated / target_area[None, :]).astype(jnp.bfloat16)  2.17 us

profile of v4, /device:TPU:0, one launch (start us, length us, event | category | flops | bytes accessed | tf_op | source)
XLA Modules:
  0.0 34.8 jit_solution(18310285630788430144)
XLA Ops:
  0.0 0.0 copy-start
  0.0 32.6 %remap.1 = f32[72,4096]{1,0:T(8,128)} custom-call(s32[8]{0:T(128)} %count.1, s32[8,512]{1,0:T(8,128)} %hbm_cells.1, bf16[72,64,128]{2,1,0:T(8,128)(2,1)} %hbm_flux.1, f32[4,8,512]{2,1,0:T(8,128)} %hbm_weight.1, f32[2,4,8,512]{3,2,1,0:T(8,128)} %hbm_offset.1, bf16[24,256]{1,0:T(8,128)(2,1)} %constant.2.clone.hbm_pattern, s32[8,512]{1,0:T(8,128)} %hbm_targets.1), custom_call_target="tpu_custom_call" | custom-call | tf_op jit(solution)/shard_map/remap/pallas_call | solution.py:295
  32.7 0.0 copy-done
  32.7 2.2 %divide_convert_fusion = bf16[72,4096]{1,0:T(8,128)(2,1)} fusion(f32[72,4096]{1,0:T(8,128)} %remap.1, f32[4096]{0:T(1024)S(1)} %copy-done), kind=kLoop, calls=%fused_computation | loop fusion | flops 589824 | bytes 1785856 | tf_op jit(solution)/shard_map/convert_element_type | solution.py:341
Async XLA Ops:
  0.0 32.7 %copy-start = (f32[4096]{0:T(1024)S(1)}, f32[4096]{0:T(1024)}, u32[]{:S(2)}) copy-start(f32[4096]{0:T(1024)} %param.14) | copy-start | bytes 49156

commit v5 on v4

--- a/solution.py
+++ b/solution.py
@@ -12,7 +12,7 @@
 LEFT = 8
 PARTS = 3
 LAG = 3
-PAIR = 2
+PAIR = 4
 LOW = 256
 
 

time: 35.1 us -> 33.1 us (0.943)
  Pallas kernels: 32.6 us -> 30.7 us
    pallas_call x1, Pallas kernels: 32.6 us -> 30.7 us  [on_device(): pl.pallas_call(remap_kernel, out_shape=jax.ShapeDtypeStruct((fields, ocea...]
where the time goes in v5:
time: 33.1 us; the launch traced here: 32.8 us
  Pallas kernels  30.7 us (93%)
  other arithmetic  2.17 us (7%)
    pallas_call x1, Pallas kernels, on_device(): pl.pallas_call(remap_kernel, out_shape=jax.ShapeDtypeStruct((fields, ocea...  30.7 us
    convert_element_type x1, other arithmetic, on_device(): return (integrated / target_area[None, :]).astype(jnp.bfloat16)  2.17 us

profile of v5, /device:TPU:0, one launch (start us, length us, event | category | flops | bytes accessed | tf_op | source)
XLA Modules:
  0.0 32.8 jit_solution(16764746832994484017)
XLA Ops:
  0.0 0.0 copy-start
  0.0 30.7 %remap.1 = f32[72,4096]{1,0:T(8,128)} custom-call(s32[8]{0:T(128)} %count.1, s32[8,512]{1,0:T(8,128)} %hbm_cells.1, bf16[72,64,128]{2,1,0:T(8,128)(2,1)} %hbm_flux.1, f32[4,8,512]{2,1,0:T(8,128)} %hbm_weight.1, f32[2,4,8,512]{3,2,1,0:T(8,128)} %hbm_offset.1, bf16[24,256]{1,0:T(8,128)(2,1)} %constant.2.clone.hbm_pattern, s32[8,512]{1,0:T(8,128)} %hbm_targets.1), custom_call_target="tpu_custom_call" | custom-call | tf_op jit(solution)/shard_map/remap/pallas_call | solution.py:295
  30.7 0.0 copy-done
  30.7 2.2 %divide_convert_fusion = bf16[72,4096]{1,0:T(8,128)(2,1)} fusion(f32[72,4096]{1,0:T(8,128)} %remap.1, f32[4096]{0:T(1024)S(1)} %copy-done), kind=kLoop, calls=%fused_computation | loop fusion | flops 589824 | bytes 1785856 | tf_op jit(solution)/shard_map/convert_element_type | solution.py:341
Async XLA Ops:
  0.0 30.7 %copy-start = (f32[4096]{0:T(1024)S(1)}, f32[4096]{0:T(1024)}, u32[]{:S(2)}) copy-start(f32[4096]{0:T(1024)} %param.14) | copy-start | bytes 49156
